TPU v7x, 32 devices: a whole 2x2x4 slice. The times are simulated.
32 devices in a mesh: segment: 2 (over x), dp: 4 (over z), mp: 4 (over y, core).
Axes of the slice: x: 2, y: 2, z: 4, core: 2. Of those that a mesh axis runs over, the one named last changes fastest.
Arguments:
- patch_tokens: bfloat16 [32, 16, 3072], P('dp', None, 'mp'), may hold values from -400 to 400
- visible_index: int32 [32, 16], P('dp'), may hold values from 0 to 63, as said below
- output_grad: bfloat16 [32, 16, 3072], P('dp', None, 'mp'), may hold values from -1.5 to 1.5
- norm_gain: float32 [2, 3072], P('segment'), may hold values from 0.1 to 1.9
- master_weights: float32 [2, 12288, 2048], P('segment', 'dp', 'mp'), may hold values from -2 to 2
- first_moment: float32 [2, 12288, 2048], P('segment', 'dp', 'mp'), may hold values from -6 to 6
- second_moment: float32 [2, 12288, 2048], P('segment', 'dp', 'mp'), may hold values from 0.01 to 1
Outputs:
- new_master: float32 [2, 12288, 2048], P('segment', 'dp', 'mp')
- new_first: float32 [2, 12288, 2048], P('segment', 'dp', 'mp')
- new_second: float32 [2, 12288, 2048], P('segment', 'dp', 'mp')
Inputs may be any that keep to these rules, and one draw needn't show every extreme that they name: `visible_index`: in each volume the 16 indices are distinct and increasing.
All inputs are finite; a program needn't handle non-finite values.
Results may differ from a plain program's by a relative error of at most 0.02.
Values may be sent and summed in bfloat16 or wider, within the bound.
A program may use at most 192 MiB of HBM per device.

v0:
```python
import math
import jax
import jax.numpy as jnp
from jax import lax
from jax.sharding import PartitionSpec as P

HD = 128
MB_VOLS = 2
beta_one = 0.9
beta_two = 0.95
learn_rate = 0.01
decay_rate = 0.1
adam_eps = 1e-08
norm_eps = 1e-05
step_count = 10


def from_behind(array, axis, by):
    peers = lax.axis_size(axis)
    pairs = [(i, i + by) for i in range(peers) if 0 <= i + by < peers]
    return lax.ppermute(array, axis, pairs)


def position_table(visible_index, model_width):
    half_width = model_width // 2
    angle_rate = jnp.exp(
        jnp.arange(half_width, dtype=jnp.float32) * (-2.0 * math.log(10000.0) / model_width)
    )
    angles = visible_index.astype(jnp.float32)[..., None] * angle_rate
    return jnp.concatenate([jnp.sin(angles), jnp.cos(angles)], axis=-1)


def norm_forward(hidden, norm_scale):
    values = hidden.astype(jnp.float32)
    centred = values - jnp.mean(values, axis=-1, keepdims=True)
    inverse_dev = lax.rsqrt(jnp.mean(centred * centred, axis=-1, keepdims=True) + norm_eps)
    standard = centred * inverse_dev
    return ((standard * norm_scale).astype(jnp.bfloat16), standard, inverse_dev)


def norm_backward(d_normed, d_output, standard, inverse_dev, norm_scale):
    scaled = d_normed * norm_scale
    inner = (
        scaled
        - jnp.mean(scaled, axis=-1, keepdims=True)
        - standard * jnp.mean(scaled * standard, axis=-1, keepdims=True)
    )
    return (d_output.astype(jnp.float32) + inner * inverse_dev).astype(jnp.bfloat16)


def softmax_rows(scores):
    lifted = jnp.exp(scores - jnp.max(scores, axis=-1, keepdims=True))
    return lifted / jnp.sum(lifted, axis=-1, keepdims=True)


def rounded(values):
    return lax.optimization_barrier(values.astype(jnp.bfloat16)).astype(jnp.float32)


def adam_update(gradient, master, first_moment, second_moment):
    new_first = beta_one * first_moment + (1.0 - beta_one) * gradient
    new_second = beta_two * second_moment + (1.0 - beta_two) * gradient * gradient
    direction = (
        new_first
        / (1.0 - beta_one**step_count)
        / (jnp.sqrt(new_second / (1.0 - beta_two**step_count)) + adam_eps)
    )
    new_master = master - learn_rate * (direction + decay_rate * master)
    return (new_master, new_first, new_second)


def layer_local(layer_in, norm_scale, weights):
    row_count, model_width = layer_in.shape
    col_count = weights.shape[1]
    head_count = col_count // HD
    length = row_count // MB_VOLS
    normed, standard, inverse_dev = norm_forward(layer_in, norm_scale)
    triple = weights[: 3 * model_width].reshape(3, model_width, col_count)
    project = jnp.einsum("nd,sdc->nsc", normed, triple, preferred_element_type=jnp.float32).astype(
        jnp.bfloat16
    )
    shaped = project.reshape(MB_VOLS, length, 3, head_count, HD)
    scores = jnp.einsum(
        "vqhe,vkhe->vhqk", shaped[:, :, 0], shaped[:, :, 1], preferred_element_type=jnp.float32
    ) * (1.0 / math.sqrt(HD))
    softmaxed = softmax_rows(scores)
    probs_half = softmaxed.astype(jnp.bfloat16)
    attended = jnp.einsum(
        "vhqk,vkhe->vqhe", probs_half, shaped[:, :, 2], preferred_element_type=jnp.float32
    )
    attended = attended.astype(jnp.bfloat16).reshape(row_count, col_count)
    return (normed, standard, inverse_dev, project, softmaxed, probs_half, attended)


def head_terms(attended, weights, model_width):
    return rounded(
        jnp.einsum(
            "nc,dc->nd", attended, weights[3 * model_width :], preferred_element_type=jnp.float32
        )
    )


def attention_back(d_output, saved_vals, weights):
    project, softmaxed, probs_half = (saved_vals[3], saved_vals[4], saved_vals[5])
    row_count, model_width = d_output.shape
    col_count = weights.shape[1]
    head_count = col_count // HD
    length = row_count // MB_VOLS
    shaped = project.reshape(MB_VOLS, length, 3, head_count, HD)
    d_attended = jnp.einsum(
        "nd,dc->nc", d_output, weights[3 * model_width :], preferred_element_type=jnp.float32
    )
    d_attended = d_attended.astype(jnp.bfloat16).reshape(MB_VOLS, length, head_count, HD)
    d_probs = jnp.einsum(
        "vqhe,vkhe->vhqk", d_attended, shaped[:, :, 2], preferred_element_type=jnp.float32
    )
    d_scores = (
        softmaxed
        * (d_probs - jnp.sum(d_probs * softmaxed, axis=-1, keepdims=True))
        * (1.0 / math.sqrt(HD))
    ).astype(jnp.bfloat16)
    d_queries = jnp.einsum(
        "vhqk,vkhe->vqhe", d_scores, shaped[:, :, 1], preferred_element_type=jnp.float32
    ).astype(jnp.bfloat16)
    d_keys = jnp.einsum(
        "vhqk,vqhe->vkhe", d_scores, shaped[:, :, 0], preferred_element_type=jnp.float32
    ).astype(jnp.bfloat16)
    d_values = jnp.einsum(
        "vhqk,vqhe->vkhe", probs_half, d_attended, preferred_element_type=jnp.float32
    ).astype(jnp.bfloat16)
    return jnp.stack([d_queries, d_keys, d_values], axis=2).reshape(row_count, 3, col_count)


def feature_terms(d_project, weights, model_width):
    col_count = weights.shape[1]
    triple = weights[: 3 * model_width].reshape(3, model_width, col_count)
    return rounded(jnp.einsum("nsc,sdc->nd", d_project, triple, preferred_element_type=jnp.float32))


def shards(
    patch_tokens, visible_index, output_grad, norm_gain, master_weights, first_moment, second_moment
):
    model_width = patch_tokens.shape[2] * lax.axis_size("mp")
    rows_here = master_weights.shape[1]
    is_first = lax.axis_index("segment") == 0
    norm_scale = norm_gain[0]
    weights = lax.all_gather(master_weights[0].astype(jnp.bfloat16), "dp", axis=0, tiled=True)
    tokens_full, grads_full = (
        lax.all_gather(patch_tokens, "mp", axis=2, tiled=True),
        lax.all_gather(output_grad, "mp", axis=2, tiled=True),
    )
    vol_count, length = visible_index.shape
    micro_count = vol_count // MB_VOLS
    mb_rows = MB_VOLS * length
    first_inputs = (
        tokens_full.astype(jnp.float32) + position_table(visible_index, model_width)
    ).astype(jnp.bfloat16)
    first_inputs = first_inputs.reshape(micro_count, mb_rows, model_width)
    out_grads = grads_full.reshape(micro_count, mb_rows, model_width)
    zeros_full = jnp.zeros((mb_rows, model_width), jnp.bfloat16)
    saved_ticks = []
    received = zeros_full
    for step_index in range(micro_count + 1):
        arriving = received
        own_input = first_inputs[step_index] if step_index < micro_count else zeros_full
        layer_in = jnp.where(is_first, own_input, arriving)
        saved_vals = layer_local(layer_in, norm_scale, weights)
        saved_ticks.append(saved_vals)
        if step_index < micro_count:
            head_part = head_terms(saved_vals[6], weights, model_width)
            mixed = lax.psum(head_part.astype(jnp.bfloat16), "mp").astype(jnp.float32)
            layer_out = (layer_in.astype(jnp.float32) + mixed).astype(jnp.bfloat16)
            received = from_behind(layer_out, "segment", 1)
    back_ticks = []
    for step_index in range(micro_count + 1):
        arriving = received if step_index > 0 else zeros_full
        own_grad = (
            out_grads[micro_count - 1 - step_index] if step_index < micro_count else zeros_full
        )
        d_output = jnp.where(is_first, arriving, own_grad)
        saved_vals = saved_ticks[micro_count - step_index]
        d_project = attention_back(d_output, saved_vals, weights)
        back_ticks.append((d_output, d_project))
        if step_index < micro_count:
            d_terms = feature_terms(d_project, weights, model_width)
            standard, inverse_dev = (saved_vals[1], saved_vals[2])
            summed = lax.psum(d_terms.astype(jnp.bfloat16), "mp").astype(jnp.float32)
            d_input = norm_backward(summed, d_output, standard, inverse_dev, norm_scale)
            received = from_behind(d_input, "segment", -1)
    all_steps = range(micro_count + 1)
    normed_ticks = jnp.stack([saved_ticks[micro_count - step_index][0] for step_index in all_steps])
    attended_ticks = jnp.stack(
        [saved_ticks[micro_count - step_index][6] for step_index in all_steps]
    )
    d_output_ticks = jnp.stack([back_ticks[step_index][0] for step_index in all_steps])
    d_project_ticks = jnp.stack([back_ticks[step_index][1] for step_index in all_steps])
    right_ticks = jnp.concatenate([d_project_ticks, attended_ticks[:, :, None]], axis=2)

    def pick_valid(ticks):
        chosen = jnp.where(is_first, ticks[1:], ticks[:-1])
        return chosen.reshape((micro_count * mb_rows,) + ticks.shape[2:])

    normed_all = pick_valid(normed_ticks)
    d_output_all = pick_valid(d_output_ticks)
    right_all = pick_valid(right_ticks)

    def one_piece(piece_index):
        first_row = piece_index * rows_here
        part_index = first_row // model_width
        col_offset = first_row % model_width
        left_norm = lax.dynamic_slice_in_dim(normed_all, col_offset, rows_here, 1)
        left_grad = lax.dynamic_slice_in_dim(d_output_all, col_offset, rows_here, 1)
        left_side = jnp.where(part_index == 3, left_grad, left_norm)
        right_side = lax.dynamic_index_in_dim(right_all, part_index, 1, keepdims=False)
        return jnp.einsum("tr,tc->rc", left_side, right_side, preferred_element_type=jnp.float32)

    blocks = lax.map(
        one_piece, jnp.arange(rows_here * lax.axis_size("dp") // rows_here, dtype=jnp.int32)
    )
    gradient = lax.psum_scatter(
        blocks.reshape(rows_here * lax.axis_size("dp"), blocks.shape[2]).astype(jnp.bfloat16),
        "dp",
        scatter_dimension=0,
        tiled=True,
    ).astype(jnp.float32)
    new_master, new_first, new_second = adam_update(
        gradient, master_weights[0], first_moment[0], second_moment[0]
    )
    return (new_master[None], new_first[None], new_second[None])


def solution(mesh):
    placed = (
        P("dp", None, "mp"),
        P("dp", None),
        P("dp", None, "mp"),
        P("segment", None),
        P("segment", "dp", "mp"),
        P("segment", "dp", "mp"),
        P("segment", "dp", "mp"),
    )
    return jax.shard_map(
        shards,
        mesh=mesh,
        in_specs=placed,
        out_specs=(P("segment", "dp", "mp"), P("segment", "dp", "mp"), P("segment", "dp", "mp")),
        check_vma=False,
    )
```

profile of v0, /device:TPU:0, one launch (start us, length us, event | category | flops | bytes accessed | tf_op | source)
XLA Modules:
  0.0 909.8 jit_solution(2568975783798834956)
XLA Ops:
  7.2 4.9 bitcast_convert_fusion
  12.3 10.1 %all_gather.10 = bf16[8,16,3072]{2,1,0:T(8,128)(2,1)S(1)} all-gather(bf16[8,16,768]{2,1,0:T(8,128)(2,1)S(1)} %copy-done.3), channel_id=1, replica_groups=mesh['segment'=2,'dp'=4,'mp'=4] {'mp'}, dimensions={2}, use_global_device_ids=true | all-gather | bytes 983040 | tf_op jit(solution)/shard_map/all_gather | solution.py:149
  22.3 2.8 multiply_sine_fusion
  25.8 207.5 %all-gather.2.cloned.1.call-done = bf16[12288,512]{1,0:T(8,128)(2,1)} async-done(((bf16[3072,512]{1,0:T(8,128)(2,1)}), bf16[12288,512]{1,0:T(8,128)(2,1)}) %all-gather.2.cloned.1.call-update) | async-done | bytes 12582928 | tf_op jit(solution)/shard_map/all_gather | solution.py:147
  233.2 5.2 slice.160
  238.5 3.6 copy-done
  242.0 1.6 convolution_convert_fusion.8
  244.9 3.6 convolution_convert_fusion.3
  248.6 30.0 %all-reduce.9.cloned.1.call-done = bf16[32,3072]{1,0:T(8,128)(2,1)} async-done(((bf16[32,3072]{1,0:T(8,128)(2,1)}), bf16[32,3072]{1,0:T(8,128)(2,1)}) %all-reduce.9.cloned.1.call-update) | async-done | bytes 196624 | tf_op jit(solution)/shard_map/psum | solution.py:171
  279.6 3.4 collective-permute-start
  283.0 3.1 collective-permute-done
  286.6 5.5 convolution_convert_fusion.7
  293.3 3.6 convolution_convert_fusion.2
  297.0 33.0 %all-reduce.11.cloned.1.call-done = bf16[32,3072]{1,0:T(8,128)(2,1)} async-done(((bf16[32,3072]{1,0:T(8,128)(2,1)}), bf16[32,3072]{1,0:T(8,128)(2,1)}) %all-reduce.11.cloned.1.call-update) | async-done | bytes 196624 | tf_op jit(solution)/shard_map/psum | solution.py:171
  330.9 3.4 collective-permute-start.1
  334.3 3.2 collective-permute-done.1
  337.9 5.5 convolution_convert_fusion.6
  344.7 3.6 convolution_convert_fusion.1
  348.4 7.8 all_gather.9
  356.2 25.1 %all-reduce.13.cloned.1.call-done = bf16[32,3072]{1,0:T(8,128)(2,1)} async-done(((bf16[32,3072]{1,0:T(8,128)(2,1)}), bf16[32,3072]{1,0:T(8,128)(2,1)}) %all-reduce.13.cloned.1.call-update) | async-done | bytes 196624 | tf_op jit(solution)/shard_map/psum | solution.py:171
  382.3 3.6 collective-permute-start.2
  386.1 2.8 collective-permute-done.2
  389.3 5.5 convolution_convert_fusion.5
  395.4 3.6 convolution_convert_fusion
  399.8 32.2 %all-reduce.15.cloned.1.call-done = bf16[32,3072]{1,0:T(8,128)(2,1)} async-done(((bf16[32,3072]{1,0:T(8,128)(2,1)}), bf16[32,3072]{1,0:T(8,128)(2,1)}) %all-reduce.15.cloned.1.call-update) | async-done | bytes 196624 | tf_op jit(solution)/shard_map/psum | solution.py:171
  433.0 3.4 collective-permute-start.3
  436.4 2.5 convolution_convert_fusion.13
  440.0 5.5 convolution_convert_fusion.4
  446.7 7.2 fusion.21
  456.2 30.7 %all-reduce.17.cloned.1.call-done = bf16[32,3072]{1,0:T(8,128)(2,1)} async-done(((bf16[32,3072]{1,0:T(8,128)(2,1)}), bf16[32,3072]{1,0:T(8,128)(2,1)}) %all-reduce.17.cloned.1.call-update) | async-done | bytes 196624 | tf_op jit(solution)/shard_map/psum | solution.py:187
  486.9 1.2 fusion.137
  488.1 1.1 fusion.125
  489.2 1.3 collective-permute-start.4
  490.5 6.2 collective-permute-done.4
  496.8 2.5 convolution_convert_fusion.12
  500.4 7.2 fusion.22
  507.7 31.0 %all-reduce.19.cloned.1.call-done = bf16[32,3072]{1,0:T(8,128)(2,1)} async-done(((bf16[32,3072]{1,0:T(8,128)(2,1)}), bf16[32,3072]{1,0:T(8,128)(2,1)}) %all-reduce.19.cloned.1.call-update) | async-done | bytes 196624 | tf_op jit(solution)/shard_map/psum | solution.py:187
  538.8 1.2 fusion.136
  540.0 1.1 fusion.104
  541.1 1.3 collective-permute-start.5
  542.4 6.2 collective-permute-done.5
  548.7 2.5 convolution_convert_fusion.11
  552.2 7.2 fusion.23
  559.6 30.9 %all-reduce.21.cloned.1.call-done = bf16[32,3072]{1,0:T(8,128)(2,1)} async-done(((bf16[32,3072]{1,0:T(8,128)(2,1)}), bf16[32,3072]{1,0:T(8,128)(2,1)}) %all-reduce.21.cloned.1.call-update) | async-done | bytes 196624 | tf_op jit(solution)/shard_map/psum | solution.py:187
  590.6 1.2 fusion.135
  591.8 1.1 fusion.111
  592.9 1.5 collective-permute-start.6
  594.5 5.9 collective-permute-done.6
  600.5 2.5 convolution_convert_fusion.10
  604.1 7.2 fusion.24
  611.4 31.0 %all-reduce.23.cloned.1.call-done = bf16[32,3072]{1,0:T(8,128)(2,1)} async-done(((bf16[32,3072]{1,0:T(8,128)(2,1)}), bf16[32,3072]{1,0:T(8,128)(2,1)}) %all-reduce.23.cloned.1.call-update) | async-done | bytes 196624 | tf_op jit(solution)/shard_map/psum | solution.py:187
  642.4 1.2 fusion.134
  643.6 1.1 fusion.118
  644.8 1.3 collective-permute-start.7
  646.3 6.1 collective-permute-done.7
  653.0 2.5 convolution_convert_fusion.9
  655.7 1.1 fusion.65
  659.7 15.8 %while.12 = (s32[]{:T(128)}, bf16[4,3072,512]{2,1,0:T(8,128)(2,1)}, s32[4]{0:T(128)S(1)}, bf16[128,3072]{1,0:T(8,128)(2,1)S(1)}, bf16[128,3072]{1,0:T(8,128)(2,1...) while((s32[]{:T(128)}, bf16[4,3072,512]{2,1,0:T(8,128)(2,1)}, ...), condition=%wide.region_42.43_spmd, body=%wide.region_41.42_spmd.sunk | while | flops 403046400 | bytes 7996187 | solution.py:217
  661.0 2.7 bitcast_dynamic-update-slice_fusion.2
  664.9 2.7 bitcast_dynamic-update-slice_fusion.2
  668.8 2.7 bitcast_dynamic-update-slice_fusion.2
  672.8 2.7 bitcast_dynamic-update-slice_fusion.2
  675.5 211.3 %reduce-scatter.2.cloned.1.call-done = bf16[3072,512]{1,0:T(8,128)(2,1)} async-done(((bf16[12288,512]{1,0:T(8,128)(2,1)}), bf16[3072,512]{1,0:T(8,128)(2,1)}) %reduce-scatter.2.cloned.1.call-update) | async-done | bytes 3145744 | tf_op jit(solution)/shard_map/reduce_scatter | solution.py:220
  886.8 16.1 %fusion.25 = (f32[1,3072,512]{2,1,0:T(8,128)}, f32[1,3072,512]{2,1,0:T(8,128)}, f32[1,3072,512]{2,1,0:T(8,128)}) fusion(bf16[3072,512]{1,0:T(8,128)(2,1)} %reduce-scatter.2.cloned.1.call-done, f32[1,3072,512]{2,1,0:T(8,128)} %param.15, f32[1,3072,512]{2,1,0:T(8,128)} %param.14, f32[1,3072,512]{2,1,0:T(8,128)} %param.13), kind=kLoop, calls=%fused_computation.39 | loop fusion | flops 25165824 | bytes 40894464 | tf_op jit(solution)/shard_map/broadcast_in_dim | solution.py:229
  (252 shorter events, 25.5 us)
Async XLA Ops:
  7.2 5.0 copy-start.27
  7.2 5.1 copy-start.3
  7.2 226.1 %all-gather.2.cloned.1.call-start = ((), (), s32[]{:S(2)}) async-start(), calls=%async_computation.1 | async-start | bytes 15728640 | tf_op jit(solution)/shard_map/all_gather | solution.py:147
  12.1 13.5 %copy-start.1 = (f32[1,3072]{1,0:T(1,128)S(1)}, f32[1,3072]{1,0:T(1,128)}, u32[]{:S(2)}) copy-start(f32[1,3072]{1,0:T(1,128)} %param.12) | copy-start | bytes 36868
  12.2 266.4 %all-reduce.9.cloned.1.call-start = ((), (), s32[]{:S(2)}) async-start(), calls=%async_computation.2 | async-start | bytes 393216 | tf_op jit(solution)/shard_map/psum | solution.py:171
  238.4 3.6 copy-start
  243.7 34.8 %copy-start.17 = (bf16[2,16,1,4,128]{4,3,1,0,2:T(4,128)(2,1)}, bf16[2,16,1,4,128]{4,3,1,0,2:T(4,128)(2,1)S(1)}, u32[]{:S(2)}) copy-start(bf16[2,16,1,4,128]{4,3,1,0,2:T(4,128)(2,1)S(1)} %get-tuple-element.136) | copy-start | bytes 98308
  243.7 35.8 %copy-start.9 = (bf16[2,16,1,4,128]{4,3,1,0,2:T(4,128)(2,1)}, bf16[2,16,1,4,128]{4,3,1,0,2:T(4,128)(2,1)S(1)}, u32[]{:S(2)}) copy-start(bf16[2,16,1,4,128]{4,3,1,0,2:T(4,128)(2,1)S(1)} %get-tuple-element.137) | copy-start | bytes 98308
  243.8 35.8 %copy-start.15 = (bf16[2,16,1,4,128]{4,3,1,0,2:T(4,128)(2,1)}, bf16[2,16,1,4,128]{4,3,1,0,2:T(4,128)(2,1)S(1)}, u32[]{:S(2)}) copy-start(bf16[2,16,1,4,128]{4,3,1,0,2:T(4,128)(2,1)S(1)} %get-tuple-element.135) | copy-start | bytes 98308
  244.6 35.0 %copy-start.30 = (f32[2,4,16]{2,1,0:T(4,128)}, f32[2,4,16]{2,1,0:T(4,128)S(1)}, u32[]{:S(2)}) copy-start(f32[2,4,16]{2,1,0:T(4,128)S(1)} %get-tuple-element.140) | copy-start | bytes 1540
  248.5 81.4 %all-reduce.11.cloned.1.call-start = ((), (), s32[]{:S(2)}) async-start(), calls=%async_computation.3 | async-start | bytes 393216 | tf_op jit(solution)/shard_map/psum | solution.py:171
  279.6 6.6 collective-permute-start
  292.1 4.9 copy-start.11
  292.1 4.9 copy-start.19
  292.1 37.8 %copy-start.21 = (bf16[2,16,1,4,128]{4,3,1,0,2:T(4,128)(2,1)}, bf16[2,16,1,4,128]{4,3,1,0,2:T(4,128)(2,1)S(1)}, u32[]{:S(2)}) copy-start(bf16[2,16,1,4,128]{4,3,1,0,2:T(4,128)(2,1)S(1)} %get-tuple-element.133) | copy-start | bytes 98308
  292.9 44.7 %copy-start.32 = (f32[2,4,16]{2,1,0:T(4,128)}, f32[2,4,16]{2,1,0:T(4,128)S(1)}, u32[]{:S(2)}) copy-start(f32[2,4,16]{2,1,0:T(4,128)S(1)} %get-tuple-element.142) | copy-start | bytes 1540
  296.9 84.4 %all-reduce.13.cloned.1.call-start = ((), (), s32[]{:S(2)}) async-start(), calls=%async_computation.4 | async-start | bytes 393216 | tf_op jit(solution)/shard_map/psum | solution.py:171
  330.9 6.6 collective-permute-start.1
  337.9 10.4 %copy-start.4 = (bf16[8,16,768]{2,1,0:T(8,128)(2,1)S(1)}, bf16[8,16,768]{2,1,0:T(8,128)(2,1)}, u32[]{:S(2)}) copy-start(bf16[8,16,768]{2,1,0:T(8,128)(2,1)} %param.11) | copy-start | bytes 589828
  343.5 0.8 copy-start.13
  343.5 38.8 %copy-start.23 = (bf16[2,16,1,4,128]{4,3,1,0,2:T(4,128)(2,1)}, bf16[2,16,1,4,128]{4,3,1,0,2:T(4,128)(2,1)S(1)}, u32[]{:S(2)}) copy-start(bf16[2,16,1,4,128]{4,3,1,0,2:T(4,128)(2,1)S(1)} %get-tuple-element.129) | copy-start | bytes 98308
  343.5 38.8 %copy-start.25 = (bf16[2,16,1,4,128]{4,3,1,0,2:T(4,128)(2,1)}, bf16[2,16,1,4,128]{4,3,1,0,2:T(4,128)(2,1)S(1)}, u32[]{:S(2)}) copy-start(bf16[2,16,1,4,128]{4,3,1,0,2:T(4,128)(2,1)S(1)} %get-tuple-element.130) | copy-start | bytes 98308
  344.3 38.0 %copy-start.34 = (f32[2,4,16]{2,1,0:T(4,128)}, f32[2,4,16]{2,1,0:T(4,128)S(1)}, u32[]{:S(2)}) copy-start(f32[2,4,16]{2,1,0:T(4,128)S(1)} %get-tuple-element.144) | copy-start | bytes 1540
  348.3 83.8 %all-reduce.15.cloned.1.call-start = ((), (), s32[]{:S(2)}) async-start(), calls=%async_computation.5 | async-start | bytes 393216 | tf_op jit(solution)/shard_map/psum | solution.py:171
  382.3 6.6 collective-permute-start.2
  399.0 87.9 %all-reduce.17.cloned.1.call-start = ((), (), s32[]{:S(2)}) async-start(), calls=%async_computation.6 | async-start | bytes 393216 | tf_op jit(solution)/shard_map/psum | solution.py:187
  433.0 6.6 collective-permute-start.3
  453.9 84.9 %all-reduce.19.cloned.1.call-start = ((), (), s32[]{:S(2)}) async-start(), calls=%async_computation.7 | async-start | bytes 393216 | tf_op jit(solution)/shard_map/psum | solution.py:187
  489.2 7.6 collective-permute-start.4
  500.3 42.1 %copy-start.6 = (bf16[1,32,1,512]{3,1,2,0:T(8,128)(2,1)S(1)}, bf16[1,32,1,512]{3,1,2,0:T(8,128)(2,1)}, u32[]{:S(2)}) copy-start(bf16[1,32,1,512]{3,1,2,0:T(8,128)(2,1)} %stack.162) | copy-start | bytes 98308
  500.3 42.1 %copy-start.7 = (bf16[1,32,1,512]{3,1,2,0:T(8,128)(2,1)S(1)}, bf16[1,32,1,512]{3,1,2,0:T(8,128)(2,1)}, u32[]{:S(2)}) copy-start(bf16[1,32,1,512]{3,1,2,0:T(8,128)(2,1)} %stack.163) | copy-start | bytes 98308
  500.3 42.1 %copy-start.8 = (bf16[1,32,1,512]{3,1,2,0:T(8,128)(2,1)S(1)}, bf16[1,32,1,512]{3,1,2,0:T(8,128)(2,1)}, u32[]{:S(2)}) copy-start(bf16[1,32,1,512]{3,1,2,0:T(8,128)(2,1)} %stack.164) | copy-start | bytes 98308
  500.4 50.9 %copy-start.14 = (bf16[2,16,1,4,128]{4,3,1,0,2:T(4,128)(2,1)S(1)}, bf16[2,16,1,4,128]{4,3,1,0,2:T(4,128)(2,1)}, u32[]{:S(2)}) copy-start(bf16[2,16,1,4,128]{4,3,1,0,2:T(4,128)(2,1)} %copy-done.13) | copy-start | bytes 98308
  500.4 51.0 %copy-start.24 = (bf16[2,16,1,4,128]{4,3,1,0,2:T(4,128)(2,1)S(1)}, bf16[2,16,1,4,128]{4,3,1,0,2:T(4,128)(2,1)}, u32[]{:S(2)}) copy-start(bf16[2,16,1,4,128]{4,3,1,0,2:T(4,128)(2,1)} %copy-done.23) | copy-start | bytes 98308
  500.4 51.0 %copy-start.29 = (f32[2,4,16,16]{2,3,1,0:T(8,128)S(1)}, f32[2,4,16,16]{2,3,1,0:T(8,128)}, u32[]{:S(2)}) copy-start(f32[2,4,16,16]{2,3,1,0:T(8,128)} %get-tuple-element.145) | copy-start | bytes 24580
  500.4 51.0 %copy-start.35 = (f32[2,4,16]{2,1,0:T(4,128)S(1)}, f32[2,4,16]{2,1,0:T(4,128)}, u32[]{:S(2)}) copy-start(f32[2,4,16]{2,1,0:T(4,128)} %copy-done.34) | copy-start | bytes 1540
  507.6 44.0 %copy-start.26 = (bf16[2,16,1,4,128]{4,3,1,0,2:T(4,128)(2,1)S(1)}, bf16[2,16,1,4,128]{4,3,1,0,2:T(4,128)(2,1)}, u32[]{:S(2)}) copy-start(bf16[2,16,1,4,128]{4,3,1,0,2:T(4,128)(2,1)} %copy-done.25) | copy-start | bytes 98308
  507.7 82.9 %all-reduce.21.cloned.1.call-start = ((), (), s32[]{:S(2)}) async-start(), calls=%async_computation.8 | async-start | bytes 393216 | tf_op jit(solution)/shard_map/psum | solution.py:187
  541.1 7.6 collective-permute-start.5
  552.2 7.3 copy-start.5
  559.4 43.6 %copy-start.12 = (bf16[2,16,1,4,128]{4,3,1,0,2:T(4,128)(2,1)S(1)}, bf16[2,16,1,4,128]{4,3,1,0,2:T(4,128)(2,1)}, u32[]{:S(2)}) copy-start(bf16[2,16,1,4,128]{4,3,1,0,2:T(4,128)(2,1)} %copy-done.11) | copy-start | bytes 98308
  559.4 43.8 %copy-start.20 = (bf16[2,16,1,4,128]{4,3,1,0,2:T(4,128)(2,1)S(1)}, bf16[2,16,1,4,128]{4,3,1,0,2:T(4,128)(2,1)}, u32[]{:S(2)}) copy-start(bf16[2,16,1,4,128]{4,3,1,0,2:T(4,128)(2,1)} %copy-done.19) | copy-start | bytes 98308
  559.4 43.8 %copy-start.28 = (f32[2,4,16,16]{2,3,1,0:T(8,128)S(1)}, f32[2,4,16,16]{2,3,1,0:T(8,128)}, u32[]{:S(2)}) copy-start(f32[2,4,16,16]{2,3,1,0:T(8,128)} %get-tuple-element.143) | copy-start | bytes 24580
  559.4 43.8 %copy-start.33 = (f32[2,4,16]{2,1,0:T(4,128)S(1)}, f32[2,4,16]{2,1,0:T(4,128)}, u32[]{:S(2)}) copy-start(f32[2,4,16]{2,1,0:T(4,128)} %copy-done.32) | copy-start | bytes 1540
  559.4 44.0 %copy-start.22 = (bf16[2,16,1,4,128]{4,3,1,0,2:T(4,128)(2,1)S(1)}, bf16[2,16,1,4,128]{4,3,1,0,2:T(4,128)(2,1)}, u32[]{:S(2)}) copy-start(bf16[2,16,1,4,128]{4,3,1,0,2:T(4,128)(2,1)} %copy-done.21) | copy-start | bytes 98308
  559.5 83.0 %all-reduce.23.cloned.1.call-start = ((), (), s32[]{:S(2)}) async-start(), calls=%async_computation.9 | async-start | bytes 393216 | tf_op jit(solution)/shard_map/psum | solution.py:187
  592.9 7.6 collective-permute-start.6
  611.3 44.3 %copy-start.10 = (bf16[2,16,1,4,128]{4,3,1,0,2:T(4,128)(2,1)S(1)}, bf16[2,16,1,4,128]{4,3,1,0,2:T(4,128)(2,1)}, u32[]{:S(2)}) copy-start(bf16[2,16,1,4,128]{4,3,1,0,2:T(4,128)(2,1)} %copy-done.9) | copy-start | bytes 98308
  611.3 44.4 %copy-start.16 = (bf16[2,16,1,4,128]{4,3,1,0,2:T(4,128)(2,1)S(1)}, bf16[2,16,1,4,128]{4,3,1,0,2:T(4,128)(2,1)}, u32[]{:S(2)}) copy-start(bf16[2,16,1,4,128]{4,3,1,0,2:T(4,128)(2,1)} %copy-done.15) | copy-start | bytes 98308
  611.3 44.4 %copy-start.31 = (f32[2,4,16]{2,1,0:T(4,128)S(1)}, f32[2,4,16]{2,1,0:T(4,128)}, u32[]{:S(2)}) copy-start(f32[2,4,16]{2,1,0:T(4,128)} %copy-done.30) | copy-start | bytes 1540
  611.3 45.6 %copy-start.18 = (bf16[2,16,1,4,128]{4,3,1,0,2:T(4,128)(2,1)S(1)}, bf16[2,16,1,4,128]{4,3,1,0,2:T(4,128)(2,1)}, u32[]{:S(2)}) copy-start(bf16[2,16,1,4,128]{4,3,1,0,2:T(4,128)(2,1)} %copy-done.17) | copy-start | bytes 98308
  611.3 275.4 %reduce-scatter.2.cloned.1.call-start = ((), (), s32[]{:S(2)}) async-start(), calls=%async_computation.10 | async-start | bytes 15728640 | tf_op jit(solution)/shard_map/reduce_scatter | solution.py:220
  644.8 7.6 collective-permute-start.7
  652.3 0.7 copy-start.2
Sparse Core Ops, SparseCore 0:
  12.3 220.9 all-gather.1
  248.7 29.8 all-reduce.8
  297.0 32.8 all-reduce.10
  348.4 32.8 all-reduce.12
  399.1 32.8 all-reduce.14
  454.0 32.8 all-reduce.16
  507.8 30.9 all-reduce.18
  559.6 30.9 all-reduce.20
  611.5 30.9 all-reduce.22
  675.6 211.1 reduce-scatter.1
where the time goes:
time: 911 us; the launch traced here: 910 us
  waiting for transfers between devices  697 us (77%)
  matrix products  100 us (11%)
  other arithmetic  41.1 us (5%)
  starting transfers between devices  19.5 us (2%)
  blocking collectives  17.9 us (2%)
  local copies, waits for them, and re-layouts  16 us (2%)
  between operations  15.4 us (2%)
    reduce_scatter x1, waiting for transfers between devices, shards(): lax.psum_scatter(blocks.reshape(rows_here * lax.axis_size('dp'), blocks.s...  211 us
    all_gather x1, waiting for transfers between devices, shards(): lax.all_gather(master_weights[0].astype(jnp.bfloat16), 'dp', axis=0, tile...  207 us
    psum x4, waiting for transfers between devices, shards(): summed = lax.psum(d_terms.astype(jnp.bfloat16), 'mp').astype(jnp.float32)  124 us
    psum x4, waiting for transfers between devices, shards(): mixed = lax.psum(head_part.astype(jnp.bfloat16), 'mp').astype(jnp.float32)  120 us
    ppermute x8, waiting for transfers between devices, from_behind(): return lax.ppermute(array, axis, pairs)  34 us
    dot_general x4, matrix products, feature_terms(): jnp.einsum('nsc,sdc->nd', d_project, triple, preferred_element_type=jnp.f...  28.8 us
    dot_general x5, matrix products, layer_local(): jnp.einsum('nd,sdc->nsc', normed, triple, preferred_element_type=jnp.floa...  23.5 us
    ppermute x8, starting transfers between devices, from_behind(): return lax.ppermute(array, axis, pairs)  19.1 us
  transfers between devices with their start and end apart: 18, of which 18 were waited for; matrix products, arithmetic and copies ran while one was open for 1% of the time, Pallas kernels for 0%

commit v1 on v0

--- a/solution.py
+++ b/solution.py
@@ -15,6 +15,24 @@
 step_count = 10
 
 
+def in_order(blocks, dim):
+    blocks = jnp.moveaxis(blocks, 0, dim)
+    dims = blocks.shape
+    return blocks.reshape(*dims[:dim], dims[dim] * dims[dim + 1], *dims[dim + 2 :])
+
+
+def doubled(x, axis):
+    size = lax.axis_size(axis)
+    blocks = x[None]
+    for level in range(size.bit_length() - 1):
+        stride = 1 << level
+        other = lax.ppermute(blocks, axis, [(i, i ^ stride) for i in range(size)])
+        both = jnp.stack([blocks, other])
+        upper = lax.axis_index(axis) >> level & 1
+        blocks = jnp.where(upper == 0, both, both[::-1]).reshape(-1, *x.shape)
+    return blocks
+
+
 def from_behind(array, axis, by):
     peers = lax.axis_size(axis)
     pairs = [(i, i + by) for i in range(peers) if 0 <= i + by < peers]
@@ -144,7 +162,8 @@
     rows_here = master_weights.shape[1]
     is_first = lax.axis_index("segment") == 0
     norm_scale = norm_gain[0]
-    weights = lax.all_gather(master_weights[0].astype(jnp.bfloat16), "dp", axis=0, tiled=True)
+    x = master_weights[0].astype(jnp.bfloat16)
+    weights = in_order(doubled(x, "dp"), 0)
     tokens_full, grads_full = (
         lax.all_gather(patch_tokens, "mp", axis=2, tiled=True),
         lax.all_gather(output_grad, "mp", axis=2, tiled=True),

time: 911 us -> 1050 us (1.15)
  waiting for transfers between devices: 697 us -> 815 us
  other arithmetic: 41.1 us -> 65.1 us
    ppermute x0 -> x2, waiting for transfers between devices: none -> 323 us  [doubled(): other = lax.ppermute(blocks, axis, [(i, i ^ stride) for i in range(size)])]
    all_gather x1 -> x0, waiting for transfers between devices: 207 us -> none  [shards(): lax.all_gather(master_weights[0].astype(jnp.bfloat16), 'dp', axis=0, tile...]
    another operation x0 -> x3, other arithmetic: none -> 13.7 us  [doubled(): both = jnp.stack([blocks, other])]
  transfers between devices with their start and end apart: 18 -> 19, of which waited for: 18 -> 19; matrix products, arithmetic and copies ran while one was open for 1% -> 1% of each run, Pallas kernels for 0% -> 0%
where the time goes in v1:
time: 1050 us
  waiting for transfers between devices  815 us (78%)
  matrix products  98.3 us (9%)
  other arithmetic  65.1 us (6%)
  starting transfers between devices  25.3 us (2%)
  blocking collectives  16.6 us (2%)
  between operations  14.8 us (1%)
  local copies, waits for them, and re-layouts  13.9 us (1%)
    ppermute x2, waiting for transfers between devices, doubled(): other = lax.ppermute(blocks, axis, [(i, i ^ stride) for i in range(size)])  323 us
    reduce_scatter x1, waiting for transfers between devices, shards(): lax.psum_scatter(blocks.reshape(rows_here * lax.axis_size('dp'), blocks.s...  211 us
    psum x4, waiting for transfers between devices, shards(): summed = lax.psum(d_terms.astype(jnp.bfloat16), 'mp').astype(jnp.float32)  125 us
    psum x4, waiting for transfers between devices, shards(): mixed = lax.psum(head_part.astype(jnp.bfloat16), 'mp').astype(jnp.float32)  124 us
    ppermute x8, waiting for transfers between devices, from_behind(): return lax.ppermute(array, axis, pairs)  32.1 us
    dot_general x4, matrix products, feature_terms(): jnp.einsum('nsc,sdc->nd', d_project, triple, preferred_element_type=jnp.f...  28.8 us
    dot_general x5, matrix products, layer_local(): jnp.einsum('nd,sdc->nsc', normed, triple, preferred_element_type=jnp.floa...  23.5 us
  transfers between devices with their start and end apart: 19, of which 19 were waited for; matrix products, arithmetic and copies ran while one was open for 1% of the time, Pallas kernels for 0%

profile of v1, /device:TPU:0, one launch (start us, length us, event | category | flops | bytes accessed | tf_op | source)
XLA Modules:
  0.0 1051.6 jit_solution(12105122791192166408)
XLA Ops:
  7.2 4.9 convert_element_type.387
  12.1 3.0 collective-permute-start
  15.1 3.2 convert_bitcast_fusion
  18.3 65.1 %collective-permute-done = bf16[1,3072,512]{2,1,0:T(8,128)(2,1)S(1)} collective-permute-done((bf16[1,3072,512]{2,1,0:T(8,128)(2,1)}, bf16[1,3072,512]{2,1,0:T(8,128)(2,1)S(1)}, u32[]{:S(2)}, u32[]{:S(2)}) %collective-permute-start) | collective-permute-done | bytes 3145760 | tf_op jit(solution)/shard_map/ppermute | solution.py:29
  83.4 1.7 copy-done.3
  85.1 2.5 pad_maximum_fusion.1
  87.6 6.5 fusion.21
  94.0 2.8 collective-permute-start.1
  96.8 8.8 all_gather.7
  105.6 2.8 multiply_sine_fusion
  109.0 257.8 %collective-permute-done.1 = bf16[2,3072,512]{2,1,0:T(8,128)(2,1)} collective-permute-done((bf16[2,3072,512]{2,1,0:T(8,128)(2,1)}, bf16[2,3072,512]{2,1,0:T(8,128)(2,1)}, u32[]{:S(2)}, u32[]{:S(2)}) %collective-permute-start.1) | collective-permute-done | bytes 6291488 | tf_op jit(solution)/shard_map/ppermute | solution.py:29
  366.8 4.7 pad_maximum_fusion
  371.5 3.6 reverse_select_fusion
  375.9 3.9 copy-done.1
  379.7 3.6 copy-done
  383.3 1.6 convolution_convert_fusion.8
  386.2 3.6 convolution_convert_fusion.3
  389.9 32.8 %all-reduce.9.cloned.1.call-done = bf16[32,3072]{1,0:T(8,128)(2,1)} async-done(((bf16[32,3072]{1,0:T(8,128)(2,1)}), bf16[32,3072]{1,0:T(8,128)(2,1)}) %all-reduce.9.cloned.1.call-update) | async-done | bytes 196624 | tf_op jit(solution)/shard_map/psum | solution.py:190
  423.6 3.4 collective-permute-start.2
  427.1 3.1 collective-permute-done.2
  430.6 5.5 convolution_convert_fusion.7
  437.3 3.6 convolution_convert_fusion.2
  441.0 33.0 %all-reduce.11.cloned.1.call-done = bf16[32,3072]{1,0:T(8,128)(2,1)} async-done(((bf16[32,3072]{1,0:T(8,128)(2,1)}), bf16[32,3072]{1,0:T(8,128)(2,1)}) %all-reduce.11.cloned.1.call-update) | async-done | bytes 196624 | tf_op jit(solution)/shard_map/psum | solution.py:190
  474.9 3.6 collective-permute-start.3
  478.5 3.0 collective-permute-done.3
  481.9 5.5 convolution_convert_fusion.6
  488.7 3.6 convolution_convert_fusion.1
  492.3 7.8 all_gather.6
  500.2 25.1 %all-reduce.13.cloned.1.call-done = bf16[32,3072]{1,0:T(8,128)(2,1)} async-done(((bf16[32,3072]{1,0:T(8,128)(2,1)}), bf16[32,3072]{1,0:T(8,128)(2,1)}) %all-reduce.13.cloned.1.call-update) | async-done | bytes 196624 | tf_op jit(solution)/shard_map/psum | solution.py:190
  526.3 3.4 collective-permute-start.4
  529.9 2.9 collective-permute-done.4
  533.3 5.5 convolution_convert_fusion.5
  539.4 3.6 convolution_convert_fusion
  543.2 32.8 %all-reduce.15.cloned.1.call-done = bf16[32,3072]{1,0:T(8,128)(2,1)} async-done(((bf16[32,3072]{1,0:T(8,128)(2,1)}), bf16[32,3072]{1,0:T(8,128)(2,1)}) %all-reduce.15.cloned.1.call-update) | async-done | bytes 196624 | tf_op jit(solution)/shard_map/psum | solution.py:190
  577.0 3.4 collective-permute-start.5
  580.4 2.5 convolution_convert_fusion.13
  583.9 5.5 convolution_convert_fusion.4
  590.6 7.2 fusion.23
  598.3 32.5 %all-reduce.17.cloned.1.call-done = bf16[32,3072]{1,0:T(8,128)(2,1)} async-done(((bf16[32,3072]{1,0:T(8,128)(2,1)}), bf16[32,3072]{1,0:T(8,128)(2,1)}) %all-reduce.17.cloned.1.call-update) | async-done | bytes 196624 | tf_op jit(solution)/shard_map/psum | solution.py:206
  633.2 1.3 collective-permute-start.6
  634.5 6.2 collective-permute-done.6
  640.8 2.5 convolution_convert_fusion.12
  644.3 7.2 fusion.24
  651.6 31.0 %all-reduce.19.cloned.1.call-done = bf16[32,3072]{1,0:T(8,128)(2,1)} async-done(((bf16[32,3072]{1,0:T(8,128)(2,1)}), bf16[32,3072]{1,0:T(8,128)(2,1)}) %all-reduce.19.cloned.1.call-update) | async-done | bytes 196624 | tf_op jit(solution)/shard_map/psum | solution.py:206
  685.0 1.5 collective-permute-start.7
  687.1 5.4 collective-permute-done.7
  692.6 2.5 convolution_convert_fusion.11
  696.1 7.2 fusion.25
  703.4 31.0 %all-reduce.21.cloned.1.call-done = bf16[32,3072]{1,0:T(8,128)(2,1)} async-done(((bf16[32,3072]{1,0:T(8,128)(2,1)}), bf16[32,3072]{1,0:T(8,128)(2,1)}) %all-reduce.21.cloned.1.call-update) | async-done | bytes 196624 | tf_op jit(solution)/shard_map/psum | solution.py:206
  736.7 1.3 collective-permute-start.8
  739.4 4.9 collective-permute-done.8
  744.3 2.5 convolution_convert_fusion.10
  747.9 7.2 fusion.26
  755.8 30.4 %all-reduce.23.cloned.1.call-done = bf16[32,3072]{1,0:T(8,128)(2,1)} async-done(((bf16[32,3072]{1,0:T(8,128)(2,1)}), bf16[32,3072]{1,0:T(8,128)(2,1)}) %all-reduce.23.cloned.1.call-update) | async-done | bytes 196624 | tf_op jit(solution)/shard_map/psum | solution.py:206
  788.6 1.3 collective-permute-start.9
  790.1 6.1 collective-permute-done.9
  796.1 2.5 convolution_convert_fusion.9
  801.8 15.8 %while.12 = (s32[]{:T(128)}, bf16[4,3072,512]{2,1,0:T(8,128)(2,1)}, s32[4]{0:T(128)S(1)}, bf16[128,3072]{1,0:T(8,128)(2,1)S(1)}, bf16[128,3072]{1,0:T(8,128)(2,1...) while((s32[]{:T(128)}, bf16[4,3072,512]{2,1,0:T(8,128)(2,1)}, ...), condition=%wide.region_42.43_spmd, body=%wide.region_41.42_spmd.sunk | while | flops 403046400 | bytes 7996187 | solution.py:236
  803.1 2.7 bitcast_dynamic-update-slice_fusion.2
  807.1 2.7 bitcast_dynamic-update-slice_fusion.2
  811.0 2.7 bitcast_dynamic-update-slice_fusion.2
  815.0 2.7 bitcast_dynamic-update-slice_fusion.2
  817.6 211.3 %reduce-scatter.2.cloned.1.call-done = bf16[3072,512]{1,0:T(8,128)(2,1)} async-done(((bf16[12288,512]{1,0:T(8,128)(2,1)}), bf16[3072,512]{1,0:T(8,128)(2,1)}) %reduce-scatter.2.cloned.1.call-update) | async-done | bytes 3145744 | tf_op jit(solution)/shard_map/reduce_scatter | solution.py:239
  1028.9 16.1 %fusion.27 = (f32[1,3072,512]{2,1,0:T(8,128)}, f32[1,3072,512]{2,1,0:T(8,128)}, f32[1,3072,512]{2,1,0:T(8,128)}) fusion(bf16[3072,512]{1,0:T(8,128)(2,1)} %reduce-scatter.2.cloned.1.call-done, f32[1,3072,512]{2,1,0:T(8,128)} %param.15, f32[1,3072,512]{2,1,0:T(8,128)} %param.14, f32[1,3072,512]{2,1,0:T(8,128)} %param.13), kind=kLoop, calls=%fused_computation.44 | loop fusion | flops 25165824 | bytes 40894464 | tf_op jit(solution)/shard_map/broadcast_in_dim | solution.py:248
  (208 shorter events, 35.0 us)
Async XLA Ops:
  7.2 415.5 %all-reduce.9.cloned.1.call-start = ((), (), s32[]{:S(2)}) async-start(), calls=%async_computation.1 | async-start | bytes 393216 | tf_op jit(solution)/shard_map/psum | solution.py:190
  12.1 71.3 %collective-permute-start = (bf16[1,3072,512]{2,1,0:T(8,128)(2,1)}, bf16[1,3072,512]{2,1,0:T(8,128)(2,1)S(1)}, u32[]{:S(2)}, u32[]{:S(2)}) collective-permute-start(bf16[1,3072,512]{2,1,0:T(8,128)(2,1)} %convert_element_type.387), channel_id=1, source_target_pairs={{0,4},{4,0},{8,12},{12,8},{1,5},{5,1},{9,13},{13,9},{2,6},{6,2},{1... | collective-permute-start | bytes 9437192 | tf_op jit(solution)/shard_map/ppermute | solution.py:29
  83.4 1.7 copy-start.3
  87.5 9.3 copy-start.7
  87.5 9.3 copy-start.5
  87.5 21.3 %copy-start.4 = (f32[1,3072]{1,0:T(1,128)S(1)}, f32[1,3072]{1,0:T(1,128)}, u32[]{:S(2)}) copy-start(f32[1,3072]{1,0:T(1,128)} %param.12) | copy-start | bytes 36868
  94.0 272.7 %collective-permute-start.1 = (bf16[2,3072,512]{2,1,0:T(8,128)(2,1)}, bf16[2,3072,512]{2,1,0:T(8,128)(2,1)}, u32[]{:S(2)}, u32[]{:S(2)}) collective-permute-start(bf16[2,3072,512]{2,1,0:T(8,128)(2,1)} %get-tuple-element.112), channel_id=1, source_target_pairs={{0,8},{4,12},{8,0},{12,4},{1,9},{5,13},{9,1},{13,5},{2,10},{6,14},... | collective-permute-start | bytes 18874376 | tf_op jit(solution)/shard_map/ppermute | solution.py:29
  96.8 270.0 %copy-start.2 = (bf16[1,2,3072,512]{3,2,1,0:T(8,128)(2,1)S(1)}, bf16[1,2,3072,512]{3,2,1,0:T(8,128)(2,1)}, u32[]{:S(2)}) copy-start(bf16[1,2,3072,512]{3,2,1,0:T(8,128)(2,1)} %get-tuple-element.111) | copy-start | bytes 18874372
  375.2 4.6 copy-start.1
  379.7 3.6 copy-start
  389.8 84.1 %all-reduce.11.cloned.1.call-start = ((), (), s32[]{:S(2)}) async-start(), calls=%async_computation.2 | async-start | bytes 393216 | tf_op jit(solution)/shard_map/psum | solution.py:190
  423.6 6.6 collective-permute-start.2
  440.9 84.4 %all-reduce.13.cloned.1.call-start = ((), (), s32[]{:S(2)}) async-start(), calls=%async_computation.3 | async-start | bytes 393216 | tf_op jit(solution)/shard_map/psum | solution.py:190
  474.9 6.6 collective-permute-start.3
  481.9 10.4 copy-start.6
  492.3 83.7 %all-reduce.15.cloned.1.call-start = ((), (), s32[]{:S(2)}) async-start(), calls=%async_computation.4 | async-start | bytes 393216 | tf_op jit(solution)/shard_map/psum | solution.py:190
  526.3 6.6 collective-permute-start.4
  543.0 87.9 %all-reduce.17.cloned.1.call-start = ((), (), s32[]{:S(2)}) async-start(), calls=%async_computation.5 | async-start | bytes 393216 | tf_op jit(solution)/shard_map/psum | solution.py:206
  577.0 6.6 collective-permute-start.5
  597.8 84.8 %all-reduce.19.cloned.1.call-start = ((), (), s32[]{:S(2)}) async-start(), calls=%async_computation.6 | async-start | bytes 393216 | tf_op jit(solution)/shard_map/psum | solution.py:206
  633.2 7.6 collective-permute-start.6
  644.3 51.0 %copy-start.10 = (f32[2,4,16,16]{2,3,1,0:T(8,128)S(1)}, f32[2,4,16,16]{2,3,1,0:T(8,128)}, u32[]{:S(2)}) copy-start(f32[2,4,16,16]{2,3,1,0:T(8,128)} %get-tuple-element.147) | copy-start | bytes 24580
  651.5 82.9 %all-reduce.21.cloned.1.call-start = ((), (), s32[]{:S(2)}) async-start(), calls=%async_computation.7 | async-start | bytes 393216 | tf_op jit(solution)/shard_map/psum | solution.py:206
  685.0 7.6 collective-permute-start.7
  703.3 43.7 %copy-start.9 = (f32[2,4,16,16]{2,3,1,0:T(8,128)S(1)}, f32[2,4,16,16]{2,3,1,0:T(8,128)}, u32[]{:S(2)}) copy-start(f32[2,4,16,16]{2,3,1,0:T(8,128)} %get-tuple-element.145) | copy-start | bytes 24580
  703.3 82.9 %all-reduce.23.cloned.1.call-start = ((), (), s32[]{:S(2)}) async-start(), calls=%async_computation.8 | async-start | bytes 393216 | tf_op jit(solution)/shard_map/psum | solution.py:206
  736.7 7.6 collective-permute-start.8
  755.1 43.7 %copy-start.8 = (f32[2,4,16,16]{2,3,1,0:T(8,128)S(1)}, f32[2,4,16,16]{2,3,1,0:T(8,128)}, u32[]{:S(2)}) copy-start(f32[2,4,16,16]{2,3,1,0:T(8,128)} %get-tuple-element.143) | copy-start | bytes 24580
  755.1 273.8 %reduce-scatter.2.cloned.1.call-start = ((), (), s32[]{:S(2)}) async-start(), calls=%async_computation.9 | async-start | bytes 15728640 | tf_op jit(solution)/shard_map/reduce_scatter | solution.py:239
  788.6 7.6 collective-permute-start.9
Sparse Core Ops, SparseCore 0:
  389.9 32.6 all-reduce.8
  441.0 32.8 all-reduce.10
  492.4 32.8 all-reduce.12
  543.1 32.8 all-reduce.14
  597.9 32.8 all-reduce.16
  651.6 30.9 all-reduce.18
  703.4 30.9 all-reduce.20
  755.3 30.9 all-reduce.22
  817.8 211.1 reduce-scatter.1
